TPU v7x, 256 devices: a whole 4x4x8 slice. The times are simulated.
256 devices in a mesh: wide: 128 (over y, z, x), narrow: 2 (over core).
Axes of the slice: x: 4, y: 4, z: 8, core: 2. Of those that a mesh axis runs over, the one named last changes fastest.
Arguments:
- genotypes: int32 [262144, 2048], P('wide', 'narrow'), may hold values from 0 to 2
- allele_means: float32 [2048], P('narrow'), may hold values from 0.6 to 1.4
- allele_scales: float32 [2048], P('narrow'), may hold values from 0.4 to 4
- test_matrix: bfloat16 [2048, 128], P('narrow'), may hold values from -0.125 to 0.125
Outputs:
- scaled_basis: float32 [262144, 128], P('wide')
- projection: float32 [2048, 128], P('narrow')
All inputs are finite; a program needn't handle non-finite values.
Results may differ from a plain program's by a relative error of at most 0.0003.
The roundings to bfloat16 on the way count: a program that leaves them out, or rounds other values in their place, can miss the bound.
Values sent between devices are 32-bit elements; how exact they have to be, the bound alone decides.
A program may use at most 64 MiB of HBM per device.

v0:
```python
import jax
import jax.numpy as jnp
from jax import lax
from jax.sharding import PartitionSpec as P


def gram_of(block):
    return lax.dot_general(block, block, (((0,), (0,)), ((), ())), precision=lax.Precision.HIGHEST)


def body(genotypes, allele_means, allele_scales, test_matrix):
    standard = (
        (genotypes.astype(jnp.float32) - allele_means[None, :]) * allele_scales[None, :]
    ).astype(jnp.bfloat16)
    partial_sketch = jnp.dot(standard, test_matrix, preferred_element_type=jnp.float32)
    sketch = lax.psum(partial_sketch, "narrow")
    gram = gram_of(sketch)
    total = lax.psum(gram, "wide")
    lower = jnp.linalg.cholesky(total)
    basis = jax.scipy.linalg.solve_triangular(lower, sketch.T, lower=True).T
    samples = genotypes.shape[0] * lax.axis_size("wide")
    scaled_basis = basis * jnp.sqrt(jnp.float32(samples))
    basis_low = basis.astype(jnp.bfloat16)
    local_term = lax.dot_general(
        standard, basis_low, (((0,), (0,)), ((), ())), preferred_element_type=jnp.float32
    )
    projection = lax.psum(local_term, "wide")
    return (scaled_basis, projection)


def solution(mesh):
    in_specs = (P("wide", "narrow"), P("narrow"), P("narrow"), P("narrow", None))
    out_specs = (P("wide", None), P("narrow", None))
    return jax.shard_map(body, mesh=mesh, in_specs=in_specs, out_specs=out_specs, check_vma=False)
```

profile of v0, /device:TPU:2, one launch (start us, length us, event | category | flops | bytes accessed | tf_op | source)
XLA Modules:
  0.0 520.2 jit_solution(7851574428624105422)
XLA Ops:
  7.2 0.0 copy-start
  7.2 0.0 copy-start.1
  7.2 0.0 copy-start.2
  7.2 0.0 all-reduce.4.cloned.1.call-start
  7.2 0.9 copy-done
  8.1 5.6 %fusion.1 = f32[2048,128]{1,0:T(8,128)} fusion(bf16[1024,128]{1,0:T(8,128)(2,1)S(1)} %copy-done, s32[2048,1024]{1,0:T(8,128)} %param.4, f32[1024]{0:T(1024)} %param.6, f32[1024]{0:T(1024)} %param.5), kind=kOutput, calls=%fused_computation.2 | convolution fusion | flops 545259520 | bytes 9707520 | tf_op jit(solution)/shard_map/dot_general | solution.py:15
  13.8 0.0 all-reduce.4.cloned.1.call-update
  13.8 0.0 all-reduce.6.cloned.1.call-start
  13.8 33.5 %all-reduce.4.cloned.1.call-done = f32[2048,128]{1,0:T(8,128)} async-done(((f32[2048,128]{1,0:T(8,128)}), f32[2048,128]{1,0:T(8,128)}) %all-reduce.4.cloned.1.call-update) | async-done | bytes 1048592 | tf_op jit(solution)/shard_map/psum | solution.py:16
  47.3 4.0 fusion.7
  51.3 0.0 all-reduce.6.cloned.1.call-update
  51.3 0.2 all-reduce.8.cloned.1.call-start
  51.5 213.0 %all-reduce.6.cloned.1.call-done = f32[128,128]{0,1:T(8,128)} async-done(((f32[128,128]{0,1:T(8,128)}), f32[128,128]{0,1:T(8,128)}) %all-reduce.6.cloned.1.call-update) | async-done | bytes 65552 | tf_op jit(solution)/shard_map/psum | solution.py:18
  264.5 0.9 copy.7
  265.4 0.9 fusion.6
  266.3 11.7 %cholesky.16 = f32[128,128]{1,0:T(8,128)S(1)} custom-call(f32[128,128]{1,0:T(8,128)S(1)} %fusion.6), custom_call_target="Cholesky" | custom-call | tf_op jit(solution)/shard_map/jit(cholesky)/cholesky | solution.py:19
  278.1 0.6 compare_reduce_fusion
  278.7 0.7 fusion.3
  279.4 9.8 %custom-call.7 = f32[1,128,128]{1,2,0:T(8,128)S(1)} custom-call(f32[1,128,128]{2,1,0:T(8,128)S(1)} %fusion.3), custom_call_target="InvertDiagBlocksLowerTriangular" | custom-call | tf_op jit(solution)/shard_map/jit(_solve_triangular)/triangular_solve | solution.py:20
  289.2 3.2 broadcast_multiply_fusion
  292.3 0.0 copy-done.1
  292.3 0.0 copy-done.2
  292.3 5.5 %fusion = f32[1024,128]{1,0:T(8,128)} fusion(s32[2048,1024]{1,0:T(8,128)} %param.4, f32[1024]{0:T(1024)S(1)} %copy-done.1, f32[1024]{0:T(1024)S(1)} %copy-done.2, bf16[2048,128]{1,0:T(8,128)(2,1)S(1)} %get-tuple-element.3), kind=kOutput, calls=%fused_computation.1 | convolution fusion | flops 545259520 | bytes 9445376 | tf_op jit(solution)/shard_map/dot_general | solution.py:24
  297.8 0.0 all-reduce.8.cloned.1.call-update
  297.9 213.9 %all-reduce.8.cloned.1.call-done = f32[1024,128]{1,0:T(8,128)} async-done(((f32[1024,128]{1,0:T(8,128)}), f32[1024,128]{1,0:T(8,128)}) %all-reduce.8.cloned.1.call-update) | async-done | bytes 524304 | tf_op jit(solution)/shard_map/psum | solution.py:27
  511.8 1.9 copy.12
  (1 shorter events, 0.0 us)
Async XLA Ops:
  7.2 1.0 copy-start
  7.2 285.2 %copy-start.1 = (f32[1024]{0:T(1024)S(1)}, f32[1024]{0:T(1024)}, u32[]{:S(2)}) copy-start(f32[1024]{0:T(1024)} %param.6) | copy-start | bytes 12292
  7.2 285.2 %copy-start.2 = (f32[1024]{0:T(1024)S(1)}, f32[1024]{0:T(1024)}, u32[]{:S(2)}) copy-start(f32[1024]{0:T(1024)} %param.5) | copy-start | bytes 12292
  7.2 40.1 %all-reduce.4.cloned.1.call-start = ((), (), s32[]{:S(2)}) async-start(), calls=%async_computation | async-start | bytes 2097152 | tf_op jit(solution)/shard_map/psum | solution.py:16
  13.8 250.7 %all-reduce.6.cloned.1.call-start = ((), (), s32[]{:S(2)}) async-start(), calls=%async_computation.1 | async-start | bytes 131072 | tf_op jit(solution)/shard_map/psum | solution.py:18
  51.3 460.5 %all-reduce.8.cloned.1.call-start = ((), (), s32[]{:S(2)}) async-start(), calls=%async_computation.2 | async-start | bytes 1048576 | tf_op jit(solution)/shard_map/psum | solution.py:27
Sparse Core Ops, SparseCore 0:
  13.9 33.3 all-reduce.3
  54.2 210.2 all-reduce.5
  298.0 213.7 all-reduce.7
where the time goes:
time: 521 us; the launch traced here: 520 us
  waiting for transfers between devices  460 us (88%)
  other arithmetic  23.7 us (5%)
  matrix products  18.3 us (4%)
  between operations  13.8 us (3%)
    psum x1, waiting for transfers between devices, body(): projection = lax.psum(local_term, 'wide')  214 us
    psum x1, waiting for transfers between devices, body(): total = lax.psum(gram, 'wide')  213 us
    psum x1, waiting for transfers between devices, body(): sketch = lax.psum(partial_sketch, 'narrow')  33.5 us
    another operation x3, other arithmetic, body(): lower = jnp.linalg.cholesky(total)  12.4 us
    another operation x2, other arithmetic, body(): basis = jax.scipy.linalg.solve_triangular(lower, sketch.T, lower=True).T  10.5 us
  transfers between devices with their start and end apart: 3, of which 3 were waited for; matrix products, arithmetic and copies ran while one was open for 0% of the time, Pallas kernels for 0%

commit v1 on v0

v1 whole, which is shorter than its diff:
```python
import functools

import jax
import jax.numpy as jnp
from jax import lax
from jax.experimental import pallas as pl
from jax.experimental.pallas import tpu as pltpu
from jax.sharding import PartitionSpec as P

NX, NY, NZ = 4, 4, 8
RANK = 128
LAG = 2
F32, BF16 = jnp.float32, jnp.bfloat16
MESH = pl.DeviceIdType.MESH
HIGHEST = lax.Precision.HIGHEST


class Place:
    def __init__(self):
        w = lax.axis_index("wide")
        self.w = w
        self.c = lax.axis_index("narrow")
        self.x = lax.rem(w, NX)
        self.z = lax.rem(lax.div(w, NX), NZ)
        self.y = lax.div(w, NX * NZ)
        self.p = self.y * NX + self.x

    def plane(self, dy, dx):
        yy, xx = lax.rem(self.y + dy, NY), lax.rem(self.x + dx, NX)
        return yy, xx, (yy * NZ + self.z) * NX + xx

    def column(self, dz):
        zz = lax.rem(self.z + dz, NZ)
        return zz, (self.y * NZ + zz) * NX + self.x


def plane_steps():
    return [(dy, dx) for dy in range(NY) for dx in range(NX)]


def far_first(n):
    return sorted(range(n), key=lambda d: -min(d, n - d))


def id_of(wide, narrow):
    return {"wide": wide, "narrow": narrow}


def remote(src, dst, send, recv, device):
    copy = pltpu.make_async_remote_copy(
        src_ref=src, dst_ref=dst, send_sem=send, recv_sem=recv, device_id=device, device_id_type=MESH
    )
    copy.start()
    return copy


def sketch_kernel(
    gen, mean, scale, test, std, sketch, gram,
    gbuf, part, other, mine, r1, r2, total,
    gsem, ps, pr, s1, v1, s2, v2, s3, v3,
):
    me = Place()
    n_chunks = gsem.shape[0]
    rows = gbuf.shape[0] // n_chunks
    plane = NX * NY
    piece = mine.shape[1]

    loads = []
    for k in range(n_chunks):
        at = pl.ds(k * rows, rows)
        copy = pltpu.make_async_copy(gen.at[at], gbuf.at[at], gsem.at[k])
        copy.start()
        loads.append(copy)

    barrier = pltpu.get_barrier_semaphore()
    pl.semaphore_signal(barrier, inc=1, device_id=id_of(me.w, 1 - me.c), device_id_type=MESH)
    for dy, dx in plane_steps()[1:]:
        _, _, w = me.plane(dy, dx)
        for core in range(2):
            pl.semaphore_signal(barrier, inc=1, device_id=id_of(w, core), device_id_type=MESH)
    for dz in range(1, NZ):
        _, w = me.column(dz)
        pl.semaphore_signal(barrier, inc=1, device_id=id_of(w, me.c), device_id_type=MESH)

    pairs = []
    acc = jnp.zeros((RANK, RANK), F32)
    for k in range(n_chunks + LAG):
        if k < n_chunks:
            at = pl.ds(k * rows, rows)
            loads[k].wait()
            std[at, :] = ((gbuf[at, :].astype(F32) - mean[...]) * scale[...]).astype(BF16)
            part[at, :] = jnp.dot(std[at, :], test[...], preferred_element_type=F32)
            if k == 0:
                pl.semaphore_wait(barrier, 1 + 2 * (plane - 1) + NZ - 1)
            pairs.append(remote(part.at[at], other.at[at], ps.at[k], pr.at[k], id_of(me.w, 1 - me.c)))
        if k >= LAG:
            at = pl.ds((k - LAG) * rows, rows)
            pairs[k - LAG].wait_recv()
            s = part[at, :] + other[at, :]
            sketch[at, :] = s
            acc += lax.dot_general(s, s, (((0,), (0,)), ((), ())), precision=HIGHEST, preferred_element_type=F32)

    for i in range(RANK // piece):
        mine[i] = acc[i * piece : (i + 1) * piece, :]
    sends = list(pairs)

    recvs = []
    for dy, dx in [(dy, dx) for dy in far_first(NY) for dx in far_first(NX)][:-1]:
        yy, xx, w = me.plane(dy, dx)
        s = dy * NX + dx
        recvs.append(remote(mine.at[plane * me.c + yy * NX + xx], r1.at[s], s1.at[s], v1.at[s], id_of(w, me.c)))
    t = mine[plane * me.c + me.p]
    for copy in recvs:
        copy.wait_recv()
    sends += recvs
    for s in range(1, plane):
        t += r1[s]
    r2[me.z] = t
    recvs = []
    for dz in far_first(NZ)[:-1]:
        _, w = me.column(dz)
        recvs.append(remote(r2.at[me.z], r2.at[me.z], s2.at[dz], v2.at[dz], id_of(w, me.c)))
    for copy in recvs:
        copy.wait_recv()
    sends += recvs
    t = r2[0]
    for i in range(1, NZ):
        t += r2[i]
    slot = plane * me.c + me.p
    total[slot] = t
    recvs = []
    for dy, dx in [(dy, dx) for dy in far_first(NY) for dx in far_first(NX)]:
        _, _, w = me.plane(dy, dx)
        for dc in range(2):
            s = (dy * NX + dx) * 2 + dc
            if s:
                core = me.c if dc == 0 else 1 - me.c
                recvs.append(remote(total.at[slot], total.at[slot], s3.at[s], v3.at[s], id_of(w, core)))
    for copy in recvs:
        copy.wait_recv()
    sends += recvs
    for i in range(RANK // piece):
        gram[i * piece : (i + 1) * piece, :] = total[i]
    for copy in sends:
        copy.wait_send()


def split3(v):
    hi = v.astype(BF16)
    rest = v - hi.astype(F32)
    mid = rest.astype(BF16)
    low = (rest - mid.astype(F32)).astype(BF16)
    return hi, mid, low


PANEL = 16


def inverse_factor(gram_ref, aug):
    n = RANK
    row = lax.broadcasted_iota(jnp.int32, (n, n), 0)
    col = lax.broadcasted_iota(jnp.int32, (n, n), 1)
    aug[:, :n] = gram_ref[...]
    aug[:, n:] = jnp.where(row == col, 1.0, 0.0).astype(F32)
    prow = lax.broadcasted_iota(jnp.int32, (PANEL, n), 0)
    prow2 = lax.broadcasted_iota(jnp.int32, (PANEL, 2 * n), 0)
    for k in range(n // PANEL):
        base = k * PANEL
        p = aug[base : base + PANEL, :]
        cols = [jnp.broadcast_to(p[:, base + j : base + j + 1], (PANEL, n)) for j in range(PANEL)]
        diag = jnp.zeros((PANEL, n), F32)
        for i in range(PANEL):
            pivot = cols[i][i : i + 1, :]
            diag = jnp.where(prow == i, pivot, diag)
            if i == PANEL - 1:
                break
            m = jnp.where(prow > i, cols[i] * (1.0 / pivot), 0.0)
            for j in range(i + 1, PANEL):
                cols[j] = cols[j] - m * cols[j][i : i + 1, :]
            m2 = jnp.concatenate([m, m], axis=1)
            p = p - m2 * p[i : i + 1, :]
        r = 1.0 / jnp.sqrt(diag)
        u = p * jnp.concatenate([r, r], axis=1)
        aug[base : base + PANEL, :] = u
        if base + PANEL < n:
            h, m, l = split3(u)
            left = jnp.concatenate([h, h, m, h, l, m], axis=0)[:, :n]
            right = jnp.concatenate([h, m, h, l, h, m], axis=0)
            upd = lax.dot_general(left, right, (((0,), (0,)), ((), ())), preferred_element_type=F32)
            aug[base + PANEL :, :] = aug[base + PANEL :, :] - upd[base + PANEL :, :]


def basis_kernel(factor, gram, sketch, scaled, low, aug):
    inverse_factor(gram, aug)
    w = aug[:, RANK:]
    basis = lax.dot_general(
        sketch[...], w, (((1,), (1,)), ((), ())), precision=HIGHEST, preferred_element_type=F32
    )
    scaled[...] = basis * factor
    low[...] = basis.astype(BF16)


def projection_kernel(std, low, out, mine, ra, sb, rb, sa, va, s2, v2, s3, v3, s4, v4):
    me = Place()
    plane = NX * NY
    piece = mine.shape[2]
    block = NX * piece
    barrier = pltpu.get_barrier_semaphore()
    for dy, dx in plane_steps()[1:]:
        _, _, w = me.plane(dy, dx)
        pl.semaphore_signal(barrier, inc=1, device_id=id_of(w, me.c), device_id_type=MESH)
    for dz in range(1, NZ):
        _, w = me.column(dz)
        pl.semaphore_signal(barrier, inc=1, device_id=id_of(w, me.c), device_id_type=MESH)

    sends, recvs = [], []
    lowt = low[...].T
    for i, dy in enumerate(far_first(NY)):
        yy = lax.rem(me.y + dy, NY)
        at = pl.ds(pl.multiple_of(yy * block, block), block)
        res = jnp.dot(lowt, std[:, at], preferred_element_type=F32)
        mine[dy] = res.T.reshape(NX, piece, RANK)
        if i == 0:
            pl.semaphore_wait(barrier, plane - 1 + NZ - 1)
        for dx in far_first(NX):
            s = dy * NX + dx
            if s:
                _, xx, w = me.plane(dy, dx)
                recvs.append(remote(mine.at[dy, xx], ra.at[s], sa.at[s], va.at[s], id_of(w, me.c)))
    t = mine[0, me.x]
    for copy in recvs:
        copy.wait_recv()
    sends += recvs
    for s in range(1, plane):
        t += ra[s]
    zp = piece // NZ
    sb[...] = t.reshape(NZ, zp, RANK)
    recvs = []
    for dz in far_first(NZ)[:-1]:
        zz, w = me.column(dz)
        recvs.append(remote(sb.at[zz], rb.at[dz], s2.at[dz], v2.at[dz], id_of(w, me.c)))
    t = sb[me.z]
    for copy in recvs:
        copy.wait_recv()
    sends += recvs
    for s in range(1, NZ):
        t += rb[s]
    first = me.p * piece
    own = pl.ds(pl.multiple_of(first + me.z * zp, zp), zp)
    out[own, :] = t
    recvs = []
    for dz in far_first(NZ)[:-1]:
        _, w = me.column(dz)
        recvs.append(remote(out.at[own], out.at[own], s3.at[dz], v3.at[dz], id_of(w, me.c)))
    for copy in recvs:
        copy.wait_recv()
    sends += recvs
    whole = pl.ds(pl.multiple_of(first, piece), piece)
    recvs = []
    for dy, dx in [(dy, dx) for dy in far_first(NY) for dx in far_first(NX)][:-1]:
        _, _, w = me.plane(dy, dx)
        s = dy * NX + dx
        recvs.append(remote(out.at[whole], out.at[whole], s4.at[s], v4.at[s], id_of(w, me.c)))
    for copy in recvs:
        copy.wait_recv()
    sends += recvs
    for copy in sends:
        copy.wait_send()


CHUNKS = 8


def body(genotypes, allele_means, allele_scales, test_matrix):
    samples, variants = genotypes.shape
    plane = NX * NY
    dma = pltpu.SemaphoreType.DMA
    vmem = pl.BlockSpec(memory_space=pltpu.VMEM)
    piece = RANK // 2 // plane
    std, sketch, gram = pl.pallas_call(
        sketch_kernel,
        out_shape=(
            jax.ShapeDtypeStruct((samples, variants), BF16),
            jax.ShapeDtypeStruct((samples, RANK), F32),
            jax.ShapeDtypeStruct((RANK, RANK), F32),
        ),
        in_specs=[pl.BlockSpec(memory_space=pltpu.HBM), vmem, vmem, vmem],
        out_specs=(vmem, vmem, vmem),
        scratch_shapes=[
            pltpu.VMEM((samples, variants), jnp.int32),
            pltpu.VMEM((samples, RANK), F32),
            pltpu.VMEM((samples, RANK), F32),
            pltpu.VMEM((RANK // piece, piece, RANK), F32),
            pltpu.VMEM((plane, piece, RANK), F32),
            pltpu.VMEM((NZ, piece, RANK), F32),
            pltpu.VMEM((RANK // piece, piece, RANK), F32),
            dma((CHUNKS,)), dma((CHUNKS,)), dma((CHUNKS,)),
            dma((plane,)), dma((plane,)), dma((NZ,)), dma((NZ,)),
            dma((2 * plane,)), dma((2 * plane,)),
        ],
        compiler_params=pltpu.CompilerParams(
            collective_id=0, has_side_effects=True, vmem_limit_bytes=40 << 20
        ),
        name="sketch_gram",
    )(genotypes, allele_means[None, :], allele_scales[None, :], test_matrix)

    factor = float(samples * lax.axis_size("wide")) ** 0.5
    scaled, low = pl.pallas_call(
        functools.partial(basis_kernel, factor),
        out_shape=(
            jax.ShapeDtypeStruct((samples, RANK), F32),
            jax.ShapeDtypeStruct((samples, RANK), BF16),
        ),
        in_specs=[vmem, vmem],
        out_specs=(vmem, vmem),
        scratch_shapes=[pltpu.VMEM((RANK, 2 * RANK), F32)],
        compiler_params=pltpu.CompilerParams(vmem_limit_bytes=40 << 20),
        name="factor_basis",
    )(gram, sketch)

    piece = variants // plane
    projection = pl.pallas_call(
        projection_kernel,
        out_shape=jax.ShapeDtypeStruct((variants, RANK), F32),
        in_specs=[vmem, vmem],
        out_specs=vmem,
        scratch_shapes=[
            pltpu.VMEM((NY, NX, piece, RANK), F32),
            pltpu.VMEM((plane, piece, RANK), F32),
            pltpu.VMEM((NZ, piece // NZ, RANK), F32),
            pltpu.VMEM((NZ, piece // NZ, RANK), F32),
            dma((plane,)), dma((plane,)), dma((NZ,)), dma((NZ,)),
            dma((NZ,)), dma((NZ,)), dma((plane,)), dma((plane,)),
        ],
        compiler_params=pltpu.CompilerParams(
            collective_id=1, has_side_effects=True, vmem_limit_bytes=40 << 20
        ),
        name="projection",
    )(std, low)
    return scaled, projection


def solution(mesh):
    in_specs = (P("wide", "narrow"), P("narrow"), P("narrow"), P("narrow", None))
    out_specs = (P("wide", None), P("narrow", None))
    return jax.shard_map(body, mesh=mesh, in_specs=in_specs, out_specs=out_specs, check_vma=False)
```

time: 521 us -> 70.6 us (0.14)
  waiting for transfers between devices: 460 us -> 0 us
  Pallas kernels: 0 us -> 63 us
  other arithmetic: 23.7 us -> 0 us
  matrix products: 18.3 us -> 0 us
  between operations: 13.8 us -> 0.66 us
    psum x3 -> x0, waiting for transfers between devices: 460 us -> none  [the longest x1 214 us: body(): projection = lax.psum(local_term, 'wide')]
    pallas_call x0 -> x3, Pallas kernels: none -> 63 us  [the longest x1 30.1 us: body(): pl.pallas_call(sketch_kernel, out_shape=(jax.ShapeDtypeStruct((samples, v...]
    another operation x5 -> x0, other arithmetic: 22.9 us -> none  [the longest x3 12.4 us: body(): lower = jnp.linalg.cholesky(total)]
    dot_general x3 -> x0, matrix products: 15.1 us -> none  [the longest x1 5.65 us: body(): jnp.dot(standard, test_matrix, preferred_element_type=jnp.float32)]
  transfers between devices with their start and end apart: 3 -> 0, of which waited for: 3 -> 0; matrix products, arithmetic and copies ran while one was open for 0% -> 0% of each run, Pallas kernels for 0% -> 0%
where the time goes in v1:
time: 70.6 us; the launch traced here: 70.2 us
  Pallas kernels  63 us (89%)
  local copies, waits for them, and re-layouts  6.49 us (9%)
    pallas_call x1, Pallas kernels, body(): pl.pallas_call(sketch_kernel, out_shape=(jax.ShapeDtypeStruct((samples, v...  30.1 us
    pallas_call x1, Pallas kernels, body(): pl.pallas_call(projection_kernel, out_shape=jax.ShapeDtypeStruct((variant...  27.4 us
    unnamed x9, local copies, waits for them, and re-layouts  6.49 us
    pallas_call x1, Pallas kernels, body(): pl.pallas_call(functools.partial(basis_kernel, factor), out_shape=(jax.Sh...  5.49 us

profile of v1, /device:TPU:2, one launch (start us, length us, event | category | flops | bytes accessed | tf_op | source)
XLA Modules:
  0.0 70.2 jit_solution(8066600668858398602)
XLA Ops:
  0.6 0.0 copy-start
  0.6 3.4 %copy-done = s32[2048,1024]{1,0:T(8,128)S(1)} copy-done((s32[2048,1024]{1,0:T(8,128)S(1)}, s32[2048,1024]{1,0:T(8,128)}, u32[]{:S(2)}) %copy-start) | copy-done | bytes 8388632
  4.0 0.0 copy-start.1
  4.0 0.9 %copy-done.1 = bf16[1024,128]{1,0:T(8,128)(2,1)S(1)} copy-done((bf16[1024,128]{1,0:T(8,128)(2,1)S(1)}, bf16[1024,128]{1,0:T(8,128)(2,1)}, u32[]{:S(2)}) %copy-start.1) | copy-done | bytes 262168
  5.0 0.0 copy-start.2
  5.0 0.7 copy-done.2
  5.7 0.0 copy-start.3
  5.7 0.7 copy-done.3
  6.3 30.1 %sketch_gram.1 = (bf16[2048,1024]{1,0:T(8,128)(2,1)S(1)}, f32[2048,128]{1,0:T(8,128)S(1)}, f32[128,128]{1,0:T(8,128)S(1)}) custom-call(s32[2048,1024]{1,0:T(8,128)S(1)} %copy-done, f32[1,1024]{1,0:T(1,128)S(1)} %bitcast.2, f32[1,1024]{1,0:T(1,128)S(1)} %bitcast.3, bf16[1024,128]{1,0:T(8,128)(2,1)S(1)} %copy-done.1), custom_call_target="tpu_custom_call" | custom-call | tf_op jit(solution)/shard_map/sketch_gram/pallas_call | solution.py:280
  36.5 5.5 %factor_basis.1 = (f32[2048,128]{1,0:T(8,128)}, bf16[2048,128]{1,0:T(8,128)(2,1)S(1)}) custom-call(f32[128,128]{1,0:T(8,128)S(1)} %get-tuple-element.7.gram, f32[2048,128]{1,0:T(8,128)S(1)} %get-tuple-element.8.sketch), custom_call_target="tpu_custom_call" | custom-call | tf_op jit(solution)/shard_map/factor_basis/pallas_call | solution.py:308
  42.0 27.4 %projection.1 = f32[1024,128]{1,0:T(8,128)S(1)} custom-call(bf16[2048,1024]{1,0:T(8,128)(2,1)S(1)} %get-tuple-element.10.std, bf16[2048,128]{1,0:T(8,128)(2,1)S(1)} %get-tuple-element.11.low), custom_call_target="tpu_custom_call" | custom-call | tf_op jit(solution)/shard_map/projection/pallas_call | solution.py:322
  69.4 0.8 %copy.7 = f32[1024,128]{1,0:T(8,128)} copy(f32[1024,128]{1,0:T(8,128)S(1)} %projection.1) | data formatting | bytes 1048576
Async XLA Ops:
  0.6 3.4 %copy-start = (s32[2048,1024]{1,0:T(8,128)S(1)}, s32[2048,1024]{1,0:T(8,128)}, u32[]{:S(2)}) copy-start(s32[2048,1024]{1,0:T(8,128)} %gen.1) | copy-start | bytes 25165828
  4.0 0.9 %copy-start.1 = (bf16[1024,128]{1,0:T(8,128)(2,1)S(1)}, bf16[1024,128]{1,0:T(8,128)(2,1)}, u32[]{:S(2)}) copy-start(bf16[1024,128]{1,0:T(8,128)(2,1)} %test.1) | copy-start | bytes 786436
  5.0 0.7 copy-start.2
  5.7 0.7 copy-start.3

commit v2 on v0

v2 whole, which is shorter than its diff:
```python
import functools

import jax
import jax.numpy as jnp
from jax import lax
from jax.experimental import pallas as pl
from jax.experimental.pallas import tpu as pltpu
from jax.sharding import PartitionSpec as P

NX, NY, NZ = 4, 4, 8
RANK = 128
CHUNKS = 8
EARLY = 5
LAG = 2
PANEL = 16
F32, BF16 = jnp.float32, jnp.bfloat16
MESH = pl.DeviceIdType.MESH
HIGHEST = lax.Precision.HIGHEST


class Place:
    def __init__(self):
        w = lax.axis_index("wide")
        self.w = w
        self.c = lax.axis_index("narrow")
        self.x = lax.rem(w, NX)
        self.z = lax.rem(lax.div(w, NX), NZ)
        self.y = lax.div(w, NX * NZ)
        self.p = self.y * NX + self.x

    def plane(self, dy, dx):
        yy, xx = lax.rem(self.y + dy, NY), lax.rem(self.x + dx, NX)
        return yy * NX + xx, {"wide": (yy * NZ + self.z) * NX + xx, "narrow": self.c}

    def column(self, dz):
        zz = lax.rem(self.z + dz, NZ)
        return zz, {"wide": (self.y * NZ + zz) * NX + self.x, "narrow": self.c}


def far_first(n):
    return sorted(range(n), key=lambda d: -min(d, n - d))


def plane_steps():
    steps = [(dy * NX + dx, dy, dx) for dy in range(NY) for dx in range(NX)]
    return sorted(steps, key=lambda s: -min(s[1], NY - s[1]) - min(s[2], NX - s[2]))[:-1]


def near_first(n):
    return far_first(n)[::-1]


def remote(src, dst, send, recv, device):
    copy = pltpu.make_async_remote_copy(
        src_ref=src, dst_ref=dst, send_sem=send, recv_sem=recv, device_id=device, device_id_type=MESH
    )
    copy.start()
    return copy


def split3(v):
    hi = v.astype(BF16)
    rest = v - hi.astype(F32)
    mid = rest.astype(BF16)
    low = (rest - mid.astype(F32)).astype(BF16)
    return hi, mid, low


def inverse_factor(aug):
    n = RANK
    prow = lax.broadcasted_iota(jnp.int32, (PANEL, n), 0)
    for k in range(n // PANEL):
        base = k * PANEL
        p = aug[base : base + PANEL, :]
        cols = [jnp.broadcast_to(p[:, base + j : base + j + 1], (PANEL, n)) for j in range(PANEL)]
        diag = jnp.zeros((PANEL, n), F32)
        for i in range(PANEL):
            pivot = cols[i][i : i + 1, :]
            diag = jnp.where(prow == i, pivot, diag)
            if i == PANEL - 1:
                break
            m = jnp.where(prow > i, cols[i] * (1.0 / pivot), 0.0)
            for j in range(i + 1, PANEL):
                cols[j] = cols[j] - m * cols[j][i : i + 1, :]
            p = p - jnp.concatenate([m, m], axis=1) * p[i : i + 1, :]
        r = 1.0 / jnp.sqrt(diag)
        u = p * jnp.concatenate([r, r], axis=1)
        aug[base : base + PANEL, :] = u
        if base + PANEL < n:
            h, m, l = split3(u)
            left = jnp.concatenate([h, h, m, h, l, m], axis=0)[:, :n]
            right = jnp.concatenate([h, m, h, l, h, m], axis=0)
            upd = lax.dot_general(left, right, (((0,), (0,)), ((), ())), preferred_element_type=F32)
            aug[base + PANEL :, :] = aug[base + PANEL :, :] - upd[base + PANEL :, :]


def main_kernel(
    factor,
    gen, mean_hbm, scale_hbm, test_hbm, scaled, out,
    gbuf, mean, scale, test, std, part, other, sketch,
    gm, r1, r2, total, aug, pm, pa, sb, rb,
    gsem, osem, ps, pr, s1, v1, s2, v2, s3, v3, s4, v4, s5, v5, s6, v6, s7, v7,
):
    me = Place()
    rows = gbuf.shape[0] // CHUNKS
    plane = NX * NY
    steps = plane_steps()
    partner = {"wide": me.w, "narrow": 1 - me.c}

    loads, operands, sends = [], [], []
    for i, (src, dst) in enumerate(((mean_hbm, mean), (scale_hbm, scale), (test_hbm, test))):
        copy = pltpu.make_async_copy(src, dst, osem.at[i])
        copy.start()
        operands.append(copy)
    for k in range(CHUNKS):
        at = pl.ds(k * rows, rows)
        copy = pltpu.make_async_copy(gen.at[at], gbuf.at[at], gsem.at[k])
        copy.start()
        loads.append(copy)

    barrier = pltpu.get_barrier_semaphore()
    for device in [me.plane(dy, dx)[1] for _, dy, dx in steps] + [
        me.column(dz)[1] for dz in far_first(NZ)[:-1]
    ] + [partner]:
        pl.semaphore_signal(barrier, inc=1, device_id=device, device_id_type=MESH)

    for copy in operands:
        copy.wait()
    pairs = []
    acc = jnp.zeros((RANK, RANK), F32)

    def exchange(k):
        at = pl.ds(k * rows, rows)
        pairs.append(remote(part.at[at], other.at[at], ps.at[k], pr.at[k], partner))

    def combine(k):
        at = pl.ds(k * rows, rows)
        pairs[k].wait_recv()
        s = part[at, :] + other[at, :]
        sketch[at, :] = s
        return lax.dot_general(s, s, (((0,), (0,)), ((), ())), precision=HIGHEST, preferred_element_type=F32)

    done = 0
    for k in range(CHUNKS):
        at = pl.ds(k * rows, rows)
        loads[k].wait()
        x = ((gbuf[at, :].astype(F32) - mean[...]) * scale[...]).astype(BF16)
        std[at, :] = x
        part[at, :] = jnp.dot(x, test[...], preferred_element_type=F32)
        if k == EARLY - 1:
            pl.semaphore_wait(barrier, plane - 1 + NZ - 1 + 1)
            for i in range(EARLY):
                exchange(i)
        elif k >= EARLY:
            exchange(k)
            if k - done >= LAG:
                acc += combine(done)
                done += 1
    while done < CHUNKS:
        acc += combine(done)
        done += 1
    sends += pairs

    gm[...] = acc.reshape(gm.shape)
    recvs = []
    for s, dy, dx in steps:
        q, device = me.plane(dy, dx)
        recvs.append(remote(gm.at[q], r1.at[s], s1.at[s], v1.at[s], device))
    t = gm[me.p]
    for copy in recvs:
        copy.wait_recv()
    sends += recvs
    for s in range(1, plane):
        t += r1[s]
    r2[me.z] = t
    recvs = []
    for dz in far_first(NZ)[:-1]:
        _, device = me.column(dz)
        recvs.append(remote(r2.at[me.z], r2.at[me.z], s2.at[dz], v2.at[dz], device))
    for copy in recvs:
        copy.wait_recv()
    sends += recvs
    t = r2[0]
    for i in range(1, NZ):
        t += r2[i]
    total[me.p] = t
    recvs = []
    for s, dy, dx in steps:
        _, device = me.plane(dy, dx)
        recvs.append(remote(total.at[me.p], total.at[me.p], s3.at[s], v3.at[s], device))
    row = lax.broadcasted_iota(jnp.int32, (RANK, RANK), 0)
    col = lax.broadcasted_iota(jnp.int32, (RANK, RANK), 1)
    aug[:, RANK:] = jnp.where(row == col, 1.0, 0.0).astype(F32)
    for copy in recvs:
        copy.wait_recv()
    sends += recvs
    aug[:, :RANK] = total[...].reshape(RANK, RANK)

    inverse_factor(aug)
    basis = lax.dot_general(
        sketch[...], aug[:, RANK:], (((1,), (1,)), ((), ())), precision=HIGHEST, preferred_element_type=F32
    )
    scaled[...] = basis * factor
    lowt = basis.astype(BF16).T

    order = near_first(NZ)
    half = NZ // 2
    stage = {}
    for g in (1, 0):
        for j in range(g * half, g * half + half, 2):
            blocks = []
            for jj in (j, j + 1):
                zz, _ = me.column(order[jj])
                blocks.append(std[:, pl.ds(pl.multiple_of(zz * RANK, RANK), RANK)])
            res = jnp.dot(lowt, jnp.concatenate(blocks, axis=1), preferred_element_type=F32).T
            pm[:, j] = res[:RANK].reshape(plane, -1, RANK)
            pm[:, j + 1] = res[RANK:].reshape(plane, -1, RANK)
        at = pl.ds(g * half, half)
        stage[g] = []
        for s, dy, dx in steps:
            q, device = me.plane(dy, dx)
            stage[g].append(remote(pm.at[q, at], pa.at[s, at], s4.at[g, s], v4.at[g, s], device))
        sends += stage[g]
    recvs = []
    for g in (1, 0):
        at = pl.ds(g * half, half)
        t = pm[me.p, at]
        for copy in stage[g]:
            copy.wait_recv()
        for s in range(1, plane):
            t += pa[s, at]
        sb[at] = t
        for j in reversed(range(max(1, g * half), g * half + half)):
            _, device = me.column(order[j])
            recvs.append(remote(sb.at[j], rb.at[j], s5.at[j], v5.at[j], device))
    for copy in recvs:
        copy.wait_recv()
    sends += recvs
    t = sb[0]
    for j in range(1, NZ):
        t += rb[j]
    out[me.p, 0] = t
    recvs = [None] * NZ
    for dz in far_first(NZ)[:-1]:
        j = order.index((NZ - dz) % NZ)
        _, device = me.column(dz)
        recvs[j] = remote(out.at[me.p, 0], out.at[me.p, j], s6.at[j], v6.at[j], device)
    sends += recvs[1:]
    last = []
    for g in (0, 1):
        at = pl.ds(g * half, half)
        for copy in recvs[max(1, g * half) : g * half + half]:
            copy.wait_recv()
        for s, dy, dx in steps:
            _, device = me.plane(dy, dx)
            last.append(remote(out.at[me.p, at], out.at[me.p, at], s7.at[g, s], v7.at[g, s], device))
    for copy in last:
        copy.wait_recv()
    sends += last
    for copy in sends:
        copy.wait_send()


def place_kernel(scaled_in, slots, scaled, projection):
    scaled[...] = scaled_in[...]
    me = Place()
    n = slots.shape[0] * slots.shape[2]
    for j, dz in enumerate(near_first(NZ)):
        zz, _ = me.column(dz)
        projection[pl.ds(pl.multiple_of(zz * n, n), n), :] = slots[:, j].reshape(n, RANK)


def body(genotypes, allele_means, allele_scales, test_matrix):
    samples, variants = genotypes.shape
    plane = NX * NY
    dma = pltpu.SemaphoreType.DMA
    vmem = pl.BlockSpec(memory_space=pltpu.VMEM)
    piece = variants // (plane * NZ)
    factor = float(samples * lax.axis_size("wide")) ** 0.5
    grow = RANK // plane
    operands = (genotypes, allele_means[None, :], allele_scales[None, :], test_matrix)
    operands = [pltpu.with_memory_space_constraint(v, pltpu.HBM) for v in operands]
    scaled, slots = pl.pallas_call(
        functools.partial(main_kernel, factor),
        out_shape=(
            jax.ShapeDtypeStruct((samples, RANK), F32),
            jax.ShapeDtypeStruct((plane, NZ, piece, RANK), F32),
        ),
        in_specs=[pl.BlockSpec(memory_space=pltpu.HBM)] * 4,
        out_specs=(vmem, vmem),
        scratch_shapes=[
            pltpu.VMEM((samples, variants), jnp.int32),
            pltpu.VMEM((1, variants), F32),
            pltpu.VMEM((1, variants), F32),
            pltpu.VMEM((variants, RANK), BF16),
            pltpu.VMEM((samples, variants), BF16),
            pltpu.VMEM((samples, RANK), F32),
            pltpu.VMEM((samples, RANK), F32),
            pltpu.VMEM((samples, RANK), F32),
            pltpu.VMEM((plane, grow, RANK), F32),
            pltpu.VMEM((plane, grow, RANK), F32),
            pltpu.VMEM((NZ, grow, RANK), F32),
            pltpu.VMEM((plane, grow, RANK), F32),
            pltpu.VMEM((RANK, 2 * RANK), F32),
            pltpu.VMEM((plane, NZ, piece, RANK), F32),
            pltpu.VMEM((plane, NZ, piece, RANK), F32),
            pltpu.VMEM((NZ, piece, RANK), F32),
            pltpu.VMEM((NZ, piece, RANK), F32),
            dma((CHUNKS,)), dma((3,)), dma((CHUNKS,)), dma((CHUNKS,)),
            dma((plane,)), dma((plane,)), dma((NZ,)), dma((NZ,)), dma((plane,)), dma((plane,)),
            dma((2, plane)), dma((2, plane)), dma((NZ,)), dma((NZ,)),
            dma((NZ,)), dma((NZ,)), dma((2, plane)), dma((2, plane)),
        ],
        compiler_params=pltpu.CompilerParams(
            collective_id=0, has_side_effects=True, vmem_limit_bytes=40 << 20
        ),
        name="sketch_factor_project",
    )(*operands)
    return pl.pallas_call(
        place_kernel,
        out_shape=(
            jax.ShapeDtypeStruct((samples, RANK), F32),
            jax.ShapeDtypeStruct((variants, RANK), F32),
        ),
        in_specs=[vmem, vmem],
        out_specs=(vmem, vmem),
        compiler_params=pltpu.CompilerParams(vmem_limit_bytes=40 << 20),
        name="place",
    )(scaled, slots)


def solution(mesh):
    in_specs = (P("wide", "narrow"), P("narrow"), P("narrow"), P("narrow", None))
    out_specs = (P("wide", None), P("narrow", None))
    return jax.shard_map(body, mesh=mesh, in_specs=in_specs, out_specs=out_specs, check_vma=False)
```

time: 521 us -> 59.4 us (0.11)
  waiting for transfers between devices: 460 us -> 0 us
  Pallas kernels: 0 us -> 58.7 us
  other arithmetic: 23.7 us -> 0 us
  matrix products: 18.3 us -> 0 us
  between operations: 13.8 us -> 0.64 us
    psum x3 -> x0, waiting for transfers between devices: 460 us -> none  [the longest x1 214 us: body(): projection = lax.psum(local_term, 'wide')]
    pallas_call x0 -> x2, Pallas kernels: none -> 58.7 us  [the longest x1 57.4 us: body(): pl.pallas_call(functools.partial(main_kernel, factor), out_shape=(jax.Sha...]
    another operation x5 -> x0, other arithmetic: 22.9 us -> none  [the longest x3 12.4 us: body(): lower = jnp.linalg.cholesky(total)]
    dot_general x3 -> x0, matrix products: 15.1 us -> none  [the longest x1 5.65 us: body(): jnp.dot(standard, test_matrix, preferred_element_type=jnp.float32)]
  transfers between devices with their start and end apart: 3 -> 0, of which waited for: 3 -> 0; matrix products, arithmetic and copies ran while one was open for 0% -> 0% of each run, Pallas kernels for 0% -> 0%
where the time goes in v2:
time: 59.4 us; the launch traced here: 59.3 us
  Pallas kernels  58.7 us (99%)
  between operations  0.64 us (1%)
    pallas_call x1, Pallas kernels, body(): pl.pallas_call(functools.partial(main_kernel, factor), out_shape=(jax.Sha...  57.4 us
    pallas_call x1, Pallas kernels, body(): pl.pallas_call(place_kernel, out_shape=(jax.ShapeDtypeStruct((samples, RA...  1.26 us

profile of v2, /device:TPU:2, one launch (start us, length us, event | category | flops | bytes accessed | tf_op | source)
XLA Modules:
  0.0 59.3 jit_solution(12486773471486862513)
XLA Ops:
  0.6 57.4 %sketch_factor_project.1 = (f32[2048,128]{1,0:T(8,128)S(1)}, f32[16,8,8,128]{3,2,1,0:T(8,128)S(1)}) custom-call(s32[2048,1024]{1,0:T(8,128)} %gen.1, f32[1,1024]{1,0:T(1,128)} %bitcast.2, f32[1,1024]{1,0:T(1,128)} %bitcast.3, bf16[1024,128]{1,0:T(8,128)(2,1)} %test_hbm.1), custom_call_target="tpu_custom_call" | custom-call | tf_op jit(solution)/shard_map/sketch_factor_project/pallas_call | solution.py:283
  58.0 1.3 %place.1 = (f32[2048,128]{1,0:T(8,128)}, f32[1024,128]{1,0:T(8,128)}) custom-call(f32[2048,128]{1,0:T(8,128)S(1)} %get-tuple-element.4.scaled_in, f32[16,8,8,128]{3,2,1,0:T(8,128)S(1)} %get-tuple-element.5.slots), custom_call_target="tpu_custom_call" | custom-call | tf_op jit(solution)/shard_map/place/pallas_call | solution.py:319

commit v3 on v2

v3 whole, which is shorter than its diff:
```python
import functools

import jax
import jax.numpy as jnp
from jax import lax
from jax.experimental import pallas as pl
from jax.experimental.pallas import tpu as pltpu
from jax.sharding import PartitionSpec as P

NX, NY, NZ = 4, 4, 8
RANK = 128
CHUNKS = 4
EARLY = 3
LAG = 2
BLOCKS = 4
AHEAD = 4
PANEL = 16
F32, BF16 = jnp.float32, jnp.bfloat16
MESH = pl.DeviceIdType.MESH
HIGHEST = lax.Precision.HIGHEST


class Place:
    def __init__(self):
        w = lax.axis_index("wide")
        self.w = w
        self.c = lax.axis_index("narrow")
        self.x = lax.rem(w, NX)
        self.z = lax.rem(lax.div(w, NX), NZ)
        self.y = lax.div(w, NX * NZ)
        self.p = self.y * NX + self.x

    def plane(self, dy, dx):
        yy, xx = lax.rem(self.y + dy, NY), lax.rem(self.x + dx, NX)
        return yy * NX + xx, {"wide": (yy * NZ + self.z) * NX + xx, "narrow": self.c}

    def column(self, dz):
        zz = lax.rem(self.z + dz, NZ)
        return zz, {"wide": (self.y * NZ + zz) * NX + self.x, "narrow": self.c}


def hops(d, n):
    return min(d, n - d)


def far_first(n):
    return sorted(range(n), key=lambda d: -hops(d, n))


def plane_steps():
    steps = [(dy * NX + dx, dy, dx) for dy in range(NY) for dx in range(NX)]
    return sorted(steps, key=lambda s: -hops(s[1], NY) - hops(s[2], NX))[:-1]


def remote(src, dst, send, recv, device):
    copy = pltpu.make_async_remote_copy(
        src_ref=src, dst_ref=dst, send_sem=send, recv_sem=recv, device_id=device, device_id_type=MESH
    )
    copy.start()
    return copy


def wait_bytes(ref, sem):
    pltpu.make_async_copy(ref, ref, sem).wait()


def split3(v):
    hi = v.astype(BF16)
    rest = v - hi.astype(F32)
    mid = rest.astype(BF16)
    low = (rest - mid.astype(F32)).astype(BF16)
    return hi, mid, low


def inverse_factor(aug):
    n = RANK
    prow = lax.broadcasted_iota(jnp.int32, (PANEL, n), 0)
    for k in range(n // PANEL):
        base = k * PANEL
        p = aug[base : base + PANEL, :]
        cols = [jnp.broadcast_to(p[:, base + j : base + j + 1], (PANEL, n)) for j in range(PANEL)]
        diag = jnp.zeros((PANEL, n), F32)
        for i in range(PANEL):
            pivot = cols[i][i : i + 1, :]
            diag = jnp.where(prow == i, pivot, diag)
            if i == PANEL - 1:
                break
            m = jnp.where(prow > i, cols[i] * (1.0 / pivot), 0.0)
            for j in range(i + 1, PANEL):
                cols[j] = cols[j] - m * cols[j][i : i + 1, :]
            p = p - jnp.concatenate([m, m], axis=1) * p[i : i + 1, :]
        r = 1.0 / jnp.sqrt(diag)
        u = p * jnp.concatenate([r, r], axis=1)
        aug[base : base + PANEL, :] = u
        if base + PANEL < n:
            h, m, l = split3(u)
            left = jnp.concatenate([h, h, m, h, l, m], axis=0)[:, :n]
            right = jnp.concatenate([h, m, h, l, h, m], axis=0)
            upd = lax.dot_general(left, right, (((0,), (0,)), ((), ())), preferred_element_type=F32)
            aug[base + PANEL :, :] = aug[base + PANEL :, :] - upd[base + PANEL :, :]


def main_kernel(
    factor,
    gen, mean_hbm, scale_hbm, test_hbm, scaled, out,
    gbuf, mean, scale, test, std, part, other, sketch,
    gm, r1, r2, total, aug, pm, pa, zb,
    gsem, osem, ps, pr, ss, rs, sa, va, sb, vb, sc, vc,
):
    me = Place()
    rows = gbuf.shape[0] // CHUNKS
    plane = NX * NY
    steps = plane_steps()
    partner = {"wide": me.w, "narrow": 1 - me.c}

    loads = []

    def load(first, last):
        for i in range(first, last):
            if i < 3:
                src, dst = ((mean_hbm, mean), (scale_hbm, scale), (test_hbm, test))[i]
                copy = pltpu.make_async_copy(src, dst, osem.at[i])
            else:
                at = pl.ds((i - 3) * rows, rows)
                copy = pltpu.make_async_copy(gen.at[at], gbuf.at[at], gsem.at[i - 3])
            copy.start()
            loads.append(copy)

    load(0, AHEAD)
    barrier = pltpu.get_barrier_semaphore()
    peers = [(hops(dy, NY) + hops(dx, NX), me.plane(dy, dx)[1]) for _, dy, dx in steps]
    peers += [(hops(dz, NZ), me.column(dz)[1]) for dz in range(1, NZ)] + [(0, partner)]
    for _, device in sorted(peers, key=lambda p: -p[0]):
        pl.semaphore_signal(barrier, inc=1, device_id=device, device_id_type=MESH)
    load(AHEAD, 3 + CHUNKS)

    for copy in loads[:3]:
        copy.wait()
    pairs = []
    acc = [jnp.zeros((2 * RANK, 2 * RANK), F32), jnp.zeros((RANK, RANK), F32)]

    def exchange(k):
        at = pl.ds(k * rows, rows)
        pairs.append(remote(part.at[at], other.at[at], ps.at[k], pr.at[k], partner))

    def combine(k):
        at = pl.ds(k * rows, rows)
        pairs[k].wait_recv()
        s = part[at, :] + other[at, :]
        sketch[at, :] = s
        h, m, l = split3(s)
        hm = jnp.concatenate([h, m], axis=1)
        acc[0] += lax.dot_general(hm, hm, (((0,), (0,)), ((), ())), preferred_element_type=F32)
        acc[1] += lax.dot_general(l, h, (((0,), (0,)), ((), ())), preferred_element_type=F32)

    done = 0
    for k in range(CHUNKS):
        at = pl.ds(k * rows, rows)
        loads[3 + k].wait()
        x = ((gbuf[at, :].astype(F32) - mean[...]) * scale[...]).astype(BF16)
        std[at, :] = x
        part[at, :] = jnp.dot(x, test[...], preferred_element_type=F32)
        if k == EARLY - 1:
            pl.semaphore_wait(barrier, plane - 1 + NZ - 1 + 1)
            for i in range(EARLY):
                exchange(i)
        elif k >= EARLY:
            exchange(k)
            if k - done >= LAG:
                combine(done)
                done += 1
    while done < CHUNKS:
        combine(done)
        done += 1

    a, b = acc
    a = a[:RANK, :RANK] + ((a[:RANK, RANK:] + a[RANK:, :RANK]) + (a[RANK:, RANK:] + (b + b.T)))
    gm[...] = a.reshape(gm.shape)
    for s, dy, dx in steps:
        q, device = me.plane(dy, dx)
        remote(gm.at[q], r1.at[s], ss.at[0], rs.at[0], device)
    t = gm[me.p]
    for copy in pairs:
        copy.wait_send()
    wait_bytes(r1.at[pl.ds(1, plane - 1)], rs.at[0])
    for s in range(1, plane):
        t += r1[s]
    r2[me.z] = t
    for dz in far_first(NZ)[:-1]:
        _, device = me.column(dz)
        remote(r2.at[me.z], r2.at[me.z], ss.at[1], rs.at[1], device)
    wait_bytes(gm.at[pl.ds(0, plane - 1)], ss.at[0])
    wait_bytes(r2.at[pl.ds(0, NZ - 1)], rs.at[1])
    t = r2[0]
    for i in range(1, NZ):
        t += r2[i]
    total[me.p] = t
    for s, dy, dx in steps:
        _, device = me.plane(dy, dx)
        remote(total.at[me.p], total.at[me.p], ss.at[2], rs.at[2], device)
    wait_bytes(r2.at[pl.ds(0, NZ - 1)], ss.at[1])
    row = lax.broadcasted_iota(jnp.int32, (RANK, RANK), 0)
    col = lax.broadcasted_iota(jnp.int32, (RANK, RANK), 1)
    aug[:, RANK:] = jnp.where(row == col, 1.0, 0.0).astype(F32)
    wait_bytes(total.at[pl.ds(0, plane - 1)], rs.at[2])
    aug[:, :RANK] = total[...].reshape(RANK, RANK)

    wait_bytes(total.at[pl.ds(0, plane - 1)], ss.at[2])

    inverse_factor(aug)
    basis = lax.dot_general(
        sketch[...], aug[:, RANK:], (((1,), (1,)), ((), ())), precision=HIGHEST, preferred_element_type=F32
    )
    scaled[...] = basis * factor
    lowt = basis.astype(BF16).T

    width = std.shape[1] // BLOCKS
    grow = width // plane
    for i in range(BLOCKS):
        res = jnp.dot(lowt, std[:, i * width : (i + 1) * width], preferred_element_type=F32)
        pm[i] = res.T.reshape(plane, grow, RANK)
        for s, dy, dx in steps:
            q, device = me.plane(dy, dx)
            remote(pm.at[i, q], pa.at[i, s], sa.at[i], va.at[i], device)
    for i in range(BLOCKS):
        t = pm[i, me.p]
        wait_bytes(pa.at[i, pl.ds(1, plane - 1)], va.at[i])
        for s in range(1, plane):
            t += pa[i, s]
        zb[i, me.z] = t
        for dz in far_first(NZ)[:-1]:
            _, device = me.column(dz)
            remote(zb.at[i, me.z], zb.at[i, me.z], sb.at[i], vb.at[i], device)
    for i in range(BLOCKS):
        wait_bytes(pm.at[i, pl.ds(0, plane - 1)], sa.at[i])
    for i in range(BLOCKS):
        wait_bytes(zb.at[i, pl.ds(0, NZ - 1)], vb.at[i])
        t = zb[i, 0]
        for z in range(1, NZ):
            t += zb[i, z]
        out[i, me.p] = t
        for s, dy, dx in steps:
            _, device = me.plane(dy, dx)
            remote(out.at[i, me.p], out.at[i, me.p], sc.at[i], vc.at[i], device)
    for i in range(BLOCKS):
        wait_bytes(zb.at[i, pl.ds(0, NZ - 1)], sb.at[i])
    for i in range(BLOCKS):
        wait_bytes(out.at[i, pl.ds(0, plane - 1)], sc.at[i])
        wait_bytes(out.at[i, pl.ds(0, plane - 1)], vc.at[i])


def place_kernel(scaled_in, projection_in, scaled, projection, sems):
    copies = [
        pltpu.make_async_copy(scaled_in, scaled, sems.at[0]),
        pltpu.make_async_copy(projection_in, projection, sems.at[1]),
    ]
    for copy in copies:
        copy.start()
    for copy in copies:
        copy.wait()


def body(genotypes, allele_means, allele_scales, test_matrix):
    samples, variants = genotypes.shape
    plane = NX * NY
    dma = pltpu.SemaphoreType.DMA
    vmem = pl.BlockSpec(memory_space=pltpu.VMEM)
    piece = variants // (plane * BLOCKS)
    factor = float(samples * lax.axis_size("wide")) ** 0.5
    grow = RANK // plane
    operands = (genotypes, allele_means[None, :], allele_scales[None, :], test_matrix)
    operands = [pltpu.with_memory_space_constraint(v, pltpu.HBM) for v in operands]
    scaled, projection = pl.pallas_call(
        functools.partial(main_kernel, factor),
        out_shape=(
            jax.ShapeDtypeStruct((samples, RANK), F32),
            jax.ShapeDtypeStruct((BLOCKS, plane, piece, RANK), F32),
        ),
        in_specs=[pl.BlockSpec(memory_space=pltpu.HBM)] * 4,
        out_specs=(vmem, vmem),
        scratch_shapes=[
            pltpu.VMEM((samples, variants), jnp.int32),
            pltpu.VMEM((1, variants), F32),
            pltpu.VMEM((1, variants), F32),
            pltpu.VMEM((variants, RANK), BF16),
            pltpu.VMEM((samples, variants), BF16),
            pltpu.VMEM((samples, RANK), F32),
            pltpu.VMEM((samples, RANK), F32),
            pltpu.VMEM((samples, RANK), F32),
            pltpu.VMEM((plane, grow, RANK), F32),
            pltpu.VMEM((plane, grow, RANK), F32),
            pltpu.VMEM((NZ, grow, RANK), F32),
            pltpu.VMEM((plane, grow, RANK), F32),
            pltpu.VMEM((RANK, 2 * RANK), F32),
            pltpu.VMEM((BLOCKS, plane, piece, RANK), F32),
            pltpu.VMEM((BLOCKS, plane, piece, RANK), F32),
            pltpu.VMEM((BLOCKS, NZ, piece, RANK), F32),
            dma((CHUNKS,)), dma((3,)), dma((CHUNKS,)), dma((CHUNKS,)),
            dma((3,)), dma((3,)), dma((BLOCKS,)), dma((BLOCKS,)),
            dma((BLOCKS,)), dma((BLOCKS,)), dma((BLOCKS,)), dma((BLOCKS,)),
        ],
        compiler_params=pltpu.CompilerParams(
            collective_id=0, has_side_effects=True, vmem_limit_bytes=40 << 20
        ),
        name="sketch_factor_project",
    )(*operands)
    return pl.pallas_call(
        place_kernel,
        out_shape=(
            jax.ShapeDtypeStruct((samples, RANK), F32),
            jax.ShapeDtypeStruct((variants, RANK), F32),
        ),
        in_specs=[vmem, vmem],
        out_specs=(pl.BlockSpec(memory_space=pltpu.HBM), pl.BlockSpec(memory_space=pltpu.HBM)),
        scratch_shapes=[dma((2,))],
        compiler_params=pltpu.CompilerParams(vmem_limit_bytes=4 << 20),
        name="place",
    )(scaled, projection.reshape(variants, RANK))


def solution(mesh):
    in_specs = (P("wide", "narrow"), P("narrow"), P("narrow"), P("narrow", None))
    out_specs = (P("wide", None), P("narrow", None))
    return jax.shard_map(body, mesh=mesh, in_specs=in_specs, out_specs=out_specs, check_vma=False)
```

time: 59.4 us -> 50 us (0.84)
  Pallas kernels: 58.7 us -> 49.2 us
    pallas_call x1, Pallas kernels: 57.4 us -> 48.1 us  [body(): pl.pallas_call(functools.partial(main_kernel, factor), out_shape=(jax.Sha...]
where the time goes in v3:
time: 50 us; the launch traced here: 49.9 us
  Pallas kernels  49.2 us (98%)
  between operations  0.64 us (1%)
    pallas_call x1, Pallas kernels, body(): pl.pallas_call(functools.partial(main_kernel, factor), out_shape=(jax.Sha...  48.1 us
    pallas_call x1, Pallas kernels, body(): pl.pallas_call(place_kernel, out_shape=(jax.ShapeDtypeStruct((samples, RA...  1.16 us

profile of v3, /device:TPU:2, one launch (start us, length us, event | category | flops | bytes accessed | tf_op | source)
XLA Modules:
  0.0 49.9 jit_solution(17224056725699562661)
XLA Ops:
  0.6 48.1 %sketch_factor_project.1 = (f32[2048,128]{1,0:T(8,128)S(1)}, f32[4,16,16,128]{3,2,1,0:T(8,128)S(1)}) custom-call(s32[2048,1024]{1,0:T(8,128)} %gen.1, f32[1,1024]{1,0:T(1,128)} %bitcast.4, f32[1,1024]{1,0:T(1,128)} %bitcast.5, bf16[1024,128]{1,0:T(8,128)(2,1)} %test_hbm.1), custom_call_target="tpu_custom_call" | custom-call | tf_op jit(solution)/shard_map/sketch_factor_project/pallas_call | solution.py:273
  48.7 1.2 %place.1 = (f32[2048,128]{1,0:T(8,128)}, f32[1024,128]{1,0:T(8,128)}) custom-call(f32[2048,128]{1,0:T(8,128)S(1)} %get-tuple-element.4.scaled_in, f32[1024,128]{1,0:T(8,128)S(1)} %bitcast.3), custom_call_target="tpu_custom_call" | custom-call | tf_op jit(solution)/shard_map/place/pallas_call | solution.py:307

commit v4 on v3

--- a/solution.py
+++ b/solution.py
@@ -9,15 +9,15 @@
 
 NX, NY, NZ = 4, 4, 8
 RANK = 128
+SIZES = (4, 4, 4, 4)
 CHUNKS = 4
 EARLY = 3
 LAG = 2
 BLOCKS = 4
-AHEAD = 4
+AHEAD = 5
 PANEL = 16
 F32, BF16 = jnp.float32, jnp.bfloat16
 MESH = pl.DeviceIdType.MESH
-HIGHEST = lax.Precision.HIGHEST
 
 
 class Place:
@@ -72,43 +72,65 @@
     return hi, mid, low
 
 
-def inverse_factor(aug):
+def contract(a, b, dim):
+    return lax.dot_general(a, b, (((dim,), (dim,)), ((), ())), preferred_element_type=F32)
+
+
+def eliminate(aug, dinv, k):
     n = RANK
+    base = k * PANEL
     prow = lax.broadcasted_iota(jnp.int32, (PANEL, n), 0)
-    for k in range(n // PANEL):
-        base = k * PANEL
-        p = aug[base : base + PANEL, :]
-        cols = [jnp.broadcast_to(p[:, base + j : base + j + 1], (PANEL, n)) for j in range(PANEL)]
-        diag = jnp.zeros((PANEL, n), F32)
-        for i in range(PANEL):
-            pivot = cols[i][i : i + 1, :]
-            diag = jnp.where(prow == i, pivot, diag)
-            if i == PANEL - 1:
-                break
-            m = jnp.where(prow > i, cols[i] * (1.0 / pivot), 0.0)
-            for j in range(i + 1, PANEL):
-                cols[j] = cols[j] - m * cols[j][i : i + 1, :]
-            p = p - jnp.concatenate([m, m], axis=1) * p[i : i + 1, :]
-        r = 1.0 / jnp.sqrt(diag)
-        u = p * jnp.concatenate([r, r], axis=1)
-        aug[base : base + PANEL, :] = u
-        if base + PANEL < n:
-            h, m, l = split3(u)
-            left = jnp.concatenate([h, h, m, h, l, m], axis=0)[:, :n]
-            right = jnp.concatenate([h, m, h, l, h, m], axis=0)
-            upd = lax.dot_general(left, right, (((0,), (0,)), ((), ())), preferred_element_type=F32)
-            aug[base + PANEL :, :] = aug[base + PANEL :, :] - upd[base + PANEL :, :]
+    p = aug[base : base + PANEL, :]
+    cols = [jnp.broadcast_to(p[:, base + j : base + j + 1], (PANEL, n)) for j in range(PANEL)]
+    inv = jnp.zeros((PANEL, n), F32)
+    for i in range(PANEL):
+        ra = 1.0 / cols[i][i : i + 1, :]
+        inv = jnp.where(prow == i, ra, inv)
+        m = cols[i] * ra
+        for j in range(i + 1, PANEL):
+            cols[j] = cols[j] - m * cols[j][i : i + 1, :]
+        m = jnp.where(prow > i, m, 0.0)
+        p = p - jnp.concatenate([m, m], axis=1) * p[i : i + 1, :]
+    aug[base : base + PANEL, n:] = p[:, n:]
+    dinv[base : base + PANEL, :] = inv
+    if base + PANEL < n:
+        h, m, l = split3(p[:, :n])
+        left = jnp.concatenate([h, h, m, h, l, m], axis=0)
+        h, m, l = split3(p * jnp.concatenate([inv, inv], axis=1))
+        right = jnp.concatenate([h, m, h, l, h, m], axis=0)
+        upd = contract(left, right, 0)
+        aug[base + PANEL :, :] = aug[base + PANEL :, :] - upd[base + PANEL :, :]
+
+
+def basis_of(hm, low, factor):
+    h, m, l = split3(factor)
+    return contract(hm[...], jnp.concatenate([h, h], axis=1), 1) + (
+        contract(hm[...], jnp.concatenate([m, m], axis=1), 1)
+        + contract(jnp.concatenate([low[...], hm[:, :RANK]], axis=1), jnp.concatenate([h, l], axis=1), 1)
+    )
+
+
+def basis_t_of(hmt, lowt, factor):
+    n = factor.shape[0]
+    h, m, l = split3(factor)
+    left = jnp.concatenate(
+        [jnp.concatenate([h, h], axis=1), jnp.concatenate([m, m], axis=1), jnp.concatenate([l, jnp.zeros_like(l)], axis=1)],
+        axis=0,
+    )
+    r = jnp.dot(left, hmt[...], preferred_element_type=F32)
+    return r[:n] + (r[n : 2 * n] + (r[2 * n :] + jnp.dot(h, lowt[...], preferred_element_type=F32)))
 
 
 def main_kernel(
     factor,
     gen, mean_hbm, scale_hbm, test_hbm, scaled, out,
-    gbuf, mean, scale, test, std, part, other, sketch,
-    gm, r1, r2, total, aug, pm, pa, zb,
+    gbuf, mean, scale, test, std, part, other, hm, low, hmt, lowt,
+    gm, r1, r2, total, aug, dinv, pm, pa, zb,
     gsem, osem, ps, pr, ss, rs, sa, va, sb, vb, sc, vc,
 ):
     me = Place()
-    rows = gbuf.shape[0] // CHUNKS
+    starts = [sum(SIZES[:k]) * gbuf.shape[0] // 16 for k in range(CHUNKS + 1)]
+    chunks = [pl.ds(a, b - a) for a, b in zip(starts, starts[1:])]
     plane = NX * NY
     steps = plane_steps()
     partner = {"wide": me.w, "narrow": 1 - me.c}
@@ -121,7 +143,7 @@
                 src, dst = ((mean_hbm, mean), (scale_hbm, scale), (test_hbm, test))[i]
                 copy = pltpu.make_async_copy(src, dst, osem.at[i])
             else:
-                at = pl.ds((i - 3) * rows, rows)
+                at = chunks[i - 3]
                 copy = pltpu.make_async_copy(gen.at[at], gbuf.at[at], gsem.at[i - 3])
             copy.start()
             loads.append(copy)
@@ -140,22 +162,21 @@
     acc = [jnp.zeros((2 * RANK, 2 * RANK), F32), jnp.zeros((RANK, RANK), F32)]
 
     def exchange(k):
-        at = pl.ds(k * rows, rows)
+        at = chunks[k]
         pairs.append(remote(part.at[at], other.at[at], ps.at[k], pr.at[k], partner))
 
     def combine(k):
-        at = pl.ds(k * rows, rows)
+        at = chunks[k]
         pairs[k].wait_recv()
         s = part[at, :] + other[at, :]
-        sketch[at, :] = s
-        h, m, l = split3(s)
-        hm = jnp.concatenate([h, m], axis=1)
-        acc[0] += lax.dot_general(hm, hm, (((0,), (0,)), ((), ())), preferred_element_type=F32)
-        acc[1] += lax.dot_general(l, h, (((0,), (0,)), ((), ())), preferred_element_type=F32)
+        h, m, low[at, :] = split3(s)
+        hm[at, :] = jnp.concatenate([h, m], axis=1)
+        acc[0] += contract(hm[at, :], hm[at, :], 0)
+        acc[1] += contract(low[at, :], h, 0)
 
     done = 0
     for k in range(CHUNKS):
-        at = pl.ds(k * rows, rows)
+        at = chunks[k]
         loads[3 + k].wait()
         x = ((gbuf[at, :].astype(F32) - mean[...]) * scale[...]).astype(BF16)
         std[at, :] = x
@@ -202,26 +223,40 @@
     row = lax.broadcasted_iota(jnp.int32, (RANK, RANK), 0)
     col = lax.broadcasted_iota(jnp.int32, (RANK, RANK), 1)
     aug[:, RANK:] = jnp.where(row == col, 1.0, 0.0).astype(F32)
+    hmt[...] = hm[...].T
+    lowt[...] = low[...].T
     wait_bytes(total.at[pl.ds(0, plane - 1)], rs.at[2])
+    wait_bytes(total.at[pl.ds(0, plane - 1)], ss.at[2])
+
     aug[:, :RANK] = total[...].reshape(RANK, RANK)
-
-    wait_bytes(total.at[pl.ds(0, plane - 1)], ss.at[2])
-
-    inverse_factor(aug)
-    basis = lax.dot_general(
-        sketch[...], aug[:, RANK:], (((1,), (1,)), ((), ())), precision=HIGHEST, preferred_element_type=F32
-    )
-    scaled[...] = basis * factor
-    lowt = basis.astype(BF16).T
-
-    width = std.shape[1] // BLOCKS
-    grow = width // plane
-    for i in range(BLOCKS):
-        res = jnp.dot(lowt, std[:, i * width : (i + 1) * width], preferred_element_type=F32)
-        pm[i] = res.T.reshape(plane, grow, RANK)
+    half = RANK // 2
+    parts = BLOCKS // 2
+    width = std.shape[1] // parts
+    grow = pm.shape[2]
+
+    def project(hf):
+        at = pl.ds(hf * half, half)
+        factor = aug[at, RANK:] * jnp.sqrt(dinv[at, :])
+        basis_low = basis_t_of(hmt, lowt, factor).astype(BF16)
+        for b in range(parts):
+            res = jnp.dot(basis_low, std[:, b * width : (b + 1) * width], preferred_element_type=F32)
+            res = jnp.concatenate([res[:, : width // 2], res[:, width // 2 :]], axis=0)
+            pm[hf * parts + b] = res.T.reshape(plane, grow, RANK)
+            send(hf * parts + b)
+
+    def send(i):
         for s, dy, dx in steps:
             q, device = me.plane(dy, dx)
             remote(pm.at[i, q], pa.at[i, s], sa.at[i], va.at[i], device)
+
+    n_panels = RANK // PANEL
+    for k in range(n_panels):
+        eliminate(aug, dinv, k)
+        if k == n_panels // 2 - 1:
+            project(0)
+    project(1)
+    scaled[...] = basis_of(hm, low, aug[:, RANK:] * jnp.sqrt(dinv[...])) * factor
+
     for i in range(BLOCKS):
         t = pm[i, me.p]
         wait_bytes(pa.at[i, pl.ds(1, plane - 1)], va.at[i])
@@ -249,15 +284,20 @@
         wait_bytes(out.at[i, pl.ds(0, plane - 1)], vc.at[i])
 
 
-def place_kernel(scaled_in, projection_in, scaled, projection, sems):
-    copies = [
-        pltpu.make_async_copy(scaled_in, scaled, sems.at[0]),
-        pltpu.make_async_copy(projection_in, projection, sems.at[1]),
-    ]
-    for copy in copies:
-        copy.start()
-    for copy in copies:
-        copy.wait()
+def place_kernel(scaled_in, blocks, scaled, projection, ordered, sems):
+    copy = pltpu.make_async_copy(scaled_in, scaled, sems.at[0])
+    copy.start()
+    parts = BLOCKS // 2
+    rows = blocks.shape[1] * blocks.shape[2]
+    first = lax.broadcasted_iota(jnp.int32, (rows, RANK), 1) < RANK // 2
+    for b in range(parts):
+        lo, hi = (blocks[i].reshape(rows, RANK) for i in (b, parts + b))
+        ordered[2 * b * rows : (2 * b + 1) * rows, :] = jnp.where(first, lo, pltpu.roll(hi, RANK // 2, 1))
+        ordered[(2 * b + 1) * rows : (2 * b + 2) * rows, :] = jnp.where(first, pltpu.roll(lo, RANK // 2, 1), hi)
+    last = pltpu.make_async_copy(ordered, projection, sems.at[1])
+    last.start()
+    copy.wait()
+    last.wait()
 
 
 def body(genotypes, allele_means, allele_scales, test_matrix):
@@ -286,12 +326,16 @@
             pltpu.VMEM((samples, variants), BF16),
             pltpu.VMEM((samples, RANK), F32),
             pltpu.VMEM((samples, RANK), F32),
-            pltpu.VMEM((samples, RANK), F32),
+            pltpu.VMEM((samples, 2 * RANK), BF16),
+            pltpu.VMEM((samples, RANK), BF16),
+            pltpu.VMEM((2 * RANK, samples), BF16),
+            pltpu.VMEM((RANK, samples), BF16),
             pltpu.VMEM((plane, grow, RANK), F32),
             pltpu.VMEM((plane, grow, RANK), F32),
             pltpu.VMEM((NZ, grow, RANK), F32),
             pltpu.VMEM((plane, grow, RANK), F32),
             pltpu.VMEM((RANK, 2 * RANK), F32),
+            pltpu.VMEM((RANK, RANK), F32),
             pltpu.VMEM((BLOCKS, plane, piece, RANK), F32),
             pltpu.VMEM((BLOCKS, plane, piece, RANK), F32),
             pltpu.VMEM((BLOCKS, NZ, piece, RANK), F32),
@@ -312,10 +356,10 @@
         ),
         in_specs=[vmem, vmem],
         out_specs=(pl.BlockSpec(memory_space=pltpu.HBM), pl.BlockSpec(memory_space=pltpu.HBM)),
-        scratch_shapes=[dma((2,))],
+        scratch_shapes=[pltpu.VMEM((variants, RANK), F32), dma((2,))],
         compiler_params=pltpu.CompilerParams(vmem_limit_bytes=4 << 20),
         name="place",
-    )(scaled, projection.reshape(variants, RANK))
+    )(scaled, projection)
 
 
 def solution(mesh):

time: 50 us -> 49 us (0.980)
  Pallas kernels: 49.2 us -> 48.3 us
    pallas_call x1, Pallas kernels: 48.1 us -> 47.1 us  [body(): pl.pallas_call(functools.partial(main_kernel, factor), out_shape=(jax.Sha...]
where the time goes in v4:
time: 49 us; the launch traced here: 48.9 us
  Pallas kernels  48.3 us (99%)
  between operations  0.64 us (1%)
    pallas_call x1, Pallas kernels, body(): pl.pallas_call(functools.partial(main_kernel, factor), out_shape=(jax.Sha...  47.1 us
    pallas_call x1, Pallas kernels, body(): pl.pallas_call(place_kernel, out_shape=(jax.ShapeDtypeStruct((samples, RA...  1.16 us

profile of v4, /device:TPU:2, one launch (start us, length us, event | category | flops | bytes accessed | tf_op | source)
XLA Modules:
  0.0 48.9 jit_solution(13693953849597922541)
XLA Ops:
  0.6 47.1 %sketch_factor_project.1 = (f32[2048,128]{1,0:T(8,128)S(1)}, f32[4,16,16,128]{3,2,1,0:T(8,128)S(1)}) custom-call(s32[2048,1024]{1,0:T(8,128)} %gen.1, f32[1,1024]{1,0:T(1,128)} %bitcast.2, f32[1,1024]{1,0:T(1,128)} %bitcast.3, bf16[1024,128]{1,0:T(8,128)(2,1)} %test_hbm.1), custom_call_target="tpu_custom_call" | custom-call | tf_op jit(solution)/shard_map/sketch_factor_project/pallas_call | solution.py:313
  47.7 1.2 %place.1 = (f32[2048,128]{1,0:T(8,128)}, f32[1024,128]{1,0:T(8,128)}) custom-call(f32[2048,128]{1,0:T(8,128)S(1)} %get-tuple-element.4.scaled_in, f32[4,16,16,128]{3,2,1,0:T(8,128)S(1)} %get-tuple-element.5.blocks), custom_call_target="tpu_custom_call" | custom-call | tf_op jit(solution)/shard_map/place/pallas_call | solution.py:351

commit v5 on v4

--- a/solution.py
+++ b/solution.py
@@ -79,27 +79,37 @@
 def eliminate(aug, dinv, k):
     n = RANK
     base = k * PANEL
-    prow = lax.broadcasted_iota(jnp.int32, (PANEL, n), 0)
-    p = aug[base : base + PANEL, :]
-    cols = [jnp.broadcast_to(p[:, base + j : base + j + 1], (PANEL, n)) for j in range(PANEL)]
-    inv = jnp.zeros((PANEL, n), F32)
+    row = lax.broadcasted_iota(jnp.int32, (8, n), 0)
+    rows = range(PANEL // 8)
+    g = [aug[base + 8 * t : base + 8 * t + 8, :n] for t in rows]
+    w = [aug[base + 8 * t : base + 8 * t + 8, n:] for t in rows]
+    cols = [[jnp.broadcast_to(v[:, base + j : base + j + 1], (8, n)) for j in range(PANEL)] for v in g]
+    inv = [jnp.zeros((8, n), F32) for _ in rows]
     for i in range(PANEL):
-        ra = 1.0 / cols[i][i : i + 1, :]
-        inv = jnp.where(prow == i, ra, inv)
-        m = cols[i] * ra
+        top, r = divmod(i, 8)
+        ra = 1.0 / cols[top][i][r : r + 1, :]
+        inv[top] = jnp.where(row == r, ra, inv[top])
+        m = {t: cols[t][i] * ra for t in rows[top:]}
         for j in range(i + 1, PANEL):
-            cols[j] = cols[j] - m * cols[j][i : i + 1, :]
-        m = jnp.where(prow > i, m, 0.0)
-        p = p - jnp.concatenate([m, m], axis=1) * p[i : i + 1, :]
-    aug[base : base + PANEL, n:] = p[:, n:]
+            pivot_row = cols[top][j][r : r + 1, :]
+            for t in rows[top:]:
+                cols[t][j] = cols[t][j] - m[t] * pivot_row
+        m[top] = jnp.where(row > r, m[top], 0.0)
+        g_row, w_row = g[top][r : r + 1, :], w[top][r : r + 1, :]
+        for t in rows[top:]:
+            g[t], w[t] = g[t] - m[t] * g_row, w[t] - m[t] * w_row
+    g, w, inv = (jnp.concatenate(v, axis=0) for v in (g, w, inv))
+    aug[base : base + PANEL, n:] = w
     dinv[base : base + PANEL, :] = inv
     if base + PANEL < n:
-        h, m, l = split3(p[:, :n])
-        left = jnp.concatenate([h, h, m, h, l, m], axis=0)
-        h, m, l = split3(p * jnp.concatenate([inv, inv], axis=1))
+        h, m, l = split3(g)
+        left = jnp.concatenate([h, h, m, h, l, m], axis=0).T
+        h, m, l = split3(jnp.concatenate([g * inv, w * inv], axis=1))
         right = jnp.concatenate([h, m, h, l, h, m], axis=0)
-        upd = contract(left, right, 0)
-        aug[base + PANEL :, :] = aug[base + PANEL :, :] - upd[base + PANEL :, :]
+        for first, last in ((base + PANEL, base + 2 * PANEL), (base + 2 * PANEL, n)):
+            if first < last:
+                upd = jnp.dot(left[first:last], right, preferred_element_type=F32)
+                aug[first:last, :] = aug[first:last, :] - upd
 
 
 def basis_of(hm, low, factor):
@@ -255,8 +265,6 @@
         if k == n_panels // 2 - 1:
             project(0)
     project(1)
-    scaled[...] = basis_of(hm, low, aug[:, RANK:] * jnp.sqrt(dinv[...])) * factor
-
     for i in range(BLOCKS):
         t = pm[i, me.p]
         wait_bytes(pa.at[i, pl.ds(1, plane - 1)], va.at[i])
@@ -266,6 +274,7 @@
         for dz in far_first(NZ)[:-1]:
             _, device = me.column(dz)
             remote(zb.at[i, me.z], zb.at[i, me.z], sb.at[i], vb.at[i], device)
+    scaled[...] = basis_of(hm, low, aug[:, RANK:] * jnp.sqrt(dinv[...])) * factor
     for i in range(BLOCKS):
         wait_bytes(pm.at[i, pl.ds(0, plane - 1)], sa.at[i])
     for i in range(BLOCKS):

time: 49 us -> 49 us (level)
  no operation moved by 1% of the time
where the time goes in v5:
time: 49 us; the launch traced here: 48.9 us
  Pallas kernels  48.2 us (98%)
  between operations  0.64 us (1%)
    pallas_call x1, Pallas kernels, body(): pl.pallas_call(functools.partial(main_kernel, factor), out_shape=(jax.Sha...  47.1 us
    pallas_call x1, Pallas kernels, body(): pl.pallas_call(place_kernel, out_shape=(jax.ShapeDtypeStruct((samples, RA...  1.16 us

profile of v5, /device:TPU:2, one launch (start us, length us, event | category | flops | bytes accessed | tf_op | source)
XLA Modules:
  0.0 48.9 jit_solution(13180843660175626052)
XLA Ops:
  0.6 47.1 %sketch_factor_project.1 = (f32[2048,128]{1,0:T(8,128)S(1)}, f32[4,16,16,128]{3,2,1,0:T(8,128)S(1)}) custom-call(s32[2048,1024]{1,0:T(8,128)} %gen.1, f32[1,1024]{1,0:T(1,128)} %bitcast.2, f32[1,1024]{1,0:T(1,128)} %bitcast.3, bf16[1024,128]{1,0:T(8,128)(2,1)} %test_hbm.1), custom_call_target="tpu_custom_call" | custom-call | tf_op jit(solution)/shard_map/sketch_factor_project/pallas_call | solution.py:322
  47.7 1.2 %place.1 = (f32[2048,128]{1,0:T(8,128)}, f32[1024,128]{1,0:T(8,128)}) custom-call(f32[2048,128]{1,0:T(8,128)S(1)} %get-tuple-element.4.scaled_in, f32[4,16,16,128]{3,2,1,0:T(8,128)S(1)} %get-tuple-element.5.blocks), custom_call_target="tpu_custom_call" | custom-call | tf_op jit(solution)/shard_map/place/pallas_call | solution.py:360

commit v6 on v5

--- a/solution.py
+++ b/solution.py
@@ -13,7 +13,7 @@
 CHUNKS = 4
 EARLY = 3
 LAG = 2
-BLOCKS = 4
+BLOCKS = 8
 AHEAD = 5
 PANEL = 16
 F32, BF16 = jnp.float32, jnp.bfloat16

time: 49 us -> 48.6 us (level)
  no operation moved by 1% of the time
where the time goes in v6:
time: 48.6 us; the launch traced here: 48.5 us
  Pallas kernels  47.9 us (99%)
  between operations  0.64 us (1%)
    pallas_call x1, Pallas kernels, body(): pl.pallas_call(functools.partial(main_kernel, factor), out_shape=(jax.Sha...  46.7 us
    pallas_call x1, Pallas kernels, body(): pl.pallas_call(place_kernel, out_shape=(jax.ShapeDtypeStruct((samples, RA...  1.16 us

profile of v6, /device:TPU:2, one launch (start us, length us, event | category | flops | bytes accessed | tf_op | source)
XLA Modules:
  0.0 48.5 jit_solution(10468765459768720944)
XLA Ops:
  0.6 46.7 %sketch_factor_project.1 = (f32[2048,128]{1,0:T(8,128)S(1)}, f32[8,16,8,128]{3,2,1,0:T(8,128)S(1)}) custom-call(s32[2048,1024]{1,0:T(8,128)} %gen.1, f32[1,1024]{1,0:T(1,128)} %bitcast.2, f32[1,1024]{1,0:T(1,128)} %bitcast.3, bf16[1024,128]{1,0:T(8,128)(2,1)} %test_hbm.1), custom_call_target="tpu_custom_call" | custom-call | tf_op jit(solution)/shard_map/sketch_factor_project/pallas_call | solution.py:322
  47.4 1.2 %place.1 = (f32[2048,128]{1,0:T(8,128)}, f32[1024,128]{1,0:T(8,128)}) custom-call(f32[2048,128]{1,0:T(8,128)S(1)} %get-tuple-element.4.scaled_in, f32[8,16,8,128]{3,2,1,0:T(8,128)S(1)} %get-tuple-element.5.blocks), custom_call_target="tpu_custom_call" | custom-call | tf_op jit(solution)/shard_map/place/pallas_call | solution.py:360
